TPU v7x, 256 devices: a whole 4x4x8 slice. The times are simulated.
256 devices in a mesh: fsdp: 16 (over x_lo, z), st: 16 (over y, x_hi, core).
Axes of the slice: x: 4 (x_hi: 2, x_lo: 2; x = x_hi * 2 + x_lo), y: 4, z: 8, core: 2. Of those that a mesh axis runs over, the one named last changes fastest.
Arguments:
- queries: bfloat16 [1, 24576, 2048], P(None, 'st', 'fsdp'), may hold values from -4.5 to 4.5
- key_rows: bfloat16 [1, 24576, 2048], P(None, 'st', 'fsdp'), may hold values from -4.5 to 4.5
- value_rows: bfloat16 [1, 24576, 2048], P(None, 'st', 'fsdp'), may hold values from -6 to 6
- out_grad: bfloat16 [1, 24576, 1536], P(None, 'st', 'fsdp'), may hold values from -6 to 6
- proj_weight: bfloat16 [2048, 1536], P('fsdp'), may hold values from -0.125 to 0.125
- pattern: int32 [64, 27], P('st'), may hold values from -1 to 63, as said below
Outputs:
- projected: bfloat16 [1, 24576, 1536], P(None, 'st', 'fsdp')
- query_grad: bfloat16 [1, 24576, 2048], P(None, 'st', 'fsdp')
- key_grad: bfloat16 [1, 24576, 2048], P(None, 'st', 'fsdp')
- value_grad: bfloat16 [1, 24576, 2048], P(None, 'st', 'fsdp')
- weight_grad: float32 [2048, 1536], P('fsdp', 'st')
Inputs may be any that keep to these rules, and one draw needn't show every extreme that they name: Slot j stands for the offsets (j // 9 - 1) in frame, (j // 3 % 3 - 1) in tile row and (j % 3 - 1) in column; pattern[t, j] is -1 or the tile at t's frame, row and column plus those offsets, which lies inside the grid of 2 frames, 16 rows and 2 columns; slots 10, 13 and 16 are never -1 where that tile exists.
All inputs are finite; a program needn't handle non-finite values.
Results may differ from a plain program's by a relative error of at most 0.023.
Values may be sent and summed in bfloat16 or wider, within the bound.
No kernel may reach another device: no remote copies, remote signals or barrier semaphores. Data moves between devices by JAX's collectives and lax.ppermute only.
A program may use at most 128 MiB of HBM per device.

v0:
```python
import jax
import jax.numpy as jnp
from jax import lax
from jax.sharding import PartitionSpec as P

HDIM = 128
TILE = 384


def with_halo(cells, sides, width):
    for axis, dim in sides:
        count = lax.axis_size(axis)
        ends = count - 1
        head = lax.slice_in_dim(cells, 0, width, axis=dim)
        tail = lax.slice_in_dim(cells, cells.shape[dim] - width, cells.shape[dim], axis=dim)
        cells = jnp.concatenate(
            [
                lax.ppermute(tail, axis, [(i, (i + 1) % count) for i in range(ends)]),
                cells,
                lax.ppermute(head, axis, [((i + 1) % count, i) for i in range(ends)]),
            ],
            axis=dim,
        )
    return cells


def shifted(block, axis, distance):
    devices = range(lax.axis_size(axis))
    route = [(i - distance, i) for i in devices if i - distance in devices]
    return lax.ppermute(block, axis, route)


def body(queries, key_rows, value_rows, out_grad, proj_weight, pattern):
    scaling = HDIM ** (-0.5)
    tok_rows = queries.shape[1]
    width_mine = queries.shape[2]
    heads_mine = width_mine // HDIM
    tiles_mine = tok_rows // TILE
    band_rows = 3 * tok_rows
    row_place = lax.axis_index("st")
    row_total = lax.axis_size("st")
    offsets = jnp.arange(3 * tiles_mine, dtype=jnp.int32)
    tile_ids = (row_place - 1) * tiles_mine + offsets
    band_row = row_place - 1 + offsets // tiles_mine
    valid = (band_row >= 0) & (band_row < row_total)
    listed = valid[None, :] & jnp.any(pattern[:, None, :] == tile_ids[None, :, None], axis=2)
    key_mask = jnp.repeat(listed, TILE, axis=1)
    stacked = jnp.stack((key_rows, value_rows))
    banded = with_halo(stacked, (("st", 2),), tok_rows)
    grad_full = lax.all_gather(out_grad, "fsdp", axis=2, tiled=True)
    back_rows = jnp.einsum(
        "vtc,kc->vtk", grad_full, proj_weight, preferred_element_type=jnp.float32
    ).astype(jnp.bfloat16)
    key_band = banded[0, 0].reshape(band_rows, heads_mine, HDIM)
    value_band = banded[1, 0].reshape(band_rows, heads_mine, HDIM)
    query_tiles = queries[0].reshape(tiles_mine, TILE, heads_mine, HDIM)
    back_tiles = back_rows[0].reshape(tiles_mine, TILE, heads_mine, HDIM)

    def one_tile(carry, items):
        query_tile, back_tile, mask_row = items
        scores = (
            jnp.einsum("ihd,khd->hik", query_tile, key_band, preferred_element_type=jnp.float32)
            * scaling
        )
        scores = jnp.where(mask_row[None, None, :], scores, -jnp.inf)
        peak_score = jnp.max(scores, axis=2, keepdims=True)
        raised = jnp.exp(scores - peak_score)
        probability = raised / jnp.sum(raised, axis=2, keepdims=True)
        weights = probability.astype(jnp.bfloat16)
        attended = jnp.einsum(
            "hik,khd->ihd", weights, value_band, preferred_element_type=jnp.float32
        ).astype(jnp.bfloat16)
        prob_grad = jnp.einsum(
            "ihd,khd->hik", back_tile, value_band, preferred_element_type=jnp.float32
        )
        row_delta = jnp.einsum(
            "ihd,ihd->hi", back_tile, attended, preferred_element_type=jnp.float32
        )
        score_grad = (probability * (prob_grad - row_delta[:, :, None])).astype(jnp.bfloat16)
        query_grad = scaling * jnp.einsum(
            "hik,khd->ihd", score_grad, key_band, preferred_element_type=jnp.float32
        )
        value_part = jnp.einsum(
            "hik,ihd->khd", weights, back_tile, preferred_element_type=jnp.float32
        )
        key_part = jnp.einsum(
            "hik,ihd->khd", score_grad, query_tile, preferred_element_type=jnp.float32
        )
        return (
            carry + jnp.stack((key_part, value_part)),
            (attended, query_grad.astype(jnp.bfloat16)),
        )

    initial = jnp.zeros((2, band_rows, heads_mine, HDIM), jnp.float32)
    band_grads, (attended, query_grad) = lax.scan(
        one_tile, initial, (query_tiles, back_tiles, key_mask)
    )
    attended_list = [attended.reshape(tok_rows, width_mine)]
    query_list = [query_grad.reshape(tok_rows, width_mine)]
    grads_list = [band_grads.reshape(2, band_rows, width_mine)]
    attended_all = jnp.stack(attended_list)
    query_out = jnp.stack(query_list)
    grads_all = jnp.stack(grads_list)
    from_above = shifted(grads_all[:, :, :tok_rows].astype(jnp.bfloat16), "st", -1).astype(
        jnp.float32
    )
    from_below = shifted(grads_all[:, :, 2 * tok_rows :].astype(jnp.bfloat16), "st", 1).astype(
        jnp.float32
    )
    own_grads = grads_all[:, :, tok_rows : 2 * tok_rows] + from_above + from_below
    key_grad = (scaling * own_grads[:, 0]).astype(jnp.bfloat16)
    value_grad = own_grads[:, 1].astype(jnp.bfloat16)
    partial_sum = jnp.einsum(
        "vtk,kc->vtc", attended_all, proj_weight, preferred_element_type=jnp.float32
    )
    projected = lax.psum_scatter(
        partial_sum.astype(jnp.bfloat16), "fsdp", scatter_dimension=2, tiled=True
    )
    weight_grad = (
        lax.psum_scatter(
            jnp.einsum(
                "vtc,vtk->ck", grad_full, attended_all, preferred_element_type=jnp.float32
            ).astype(jnp.bfloat16),
            "st",
            scatter_dimension=0,
            tiled=True,
        )
        .astype(jnp.float32)
        .T
    )
    return (projected, query_out, key_grad, value_grad, weight_grad)


def solution(mesh):
    in_specs = (
        P(None, "st", "fsdp"),
        P(None, "st", "fsdp"),
        P(None, "st", "fsdp"),
        P(None, "st", "fsdp"),
        P("fsdp", None),
        P("st", None),
    )
    out_specs = (
        P(None, "st", "fsdp"),
        P(None, "st", "fsdp"),
        P(None, "st", "fsdp"),
        P(None, "st", "fsdp"),
        P("fsdp", "st"),
    )
    return jax.shard_map(body, mesh=mesh, in_specs=in_specs, out_specs=out_specs, check_vma=False)
```

profile of v0, /device:TPU:2, one launch (start us, length us, event | category | flops | bytes accessed | tf_op | source)
XLA Modules:
  0.0 352.4 jit_solution(13838236527332941068)
XLA Ops:
  8.0 1.2 pad_maximum_fusion.1
  9.2 1.3 collective-permute-start.1
  10.5 3.1 collective-permute-start
  13.6 1.0 compare_reduce_fusion
  15.4 1.3 pad_maximum_fusion
  16.8 72.5 %all-gather.2.cloned.1.call-done = bf16[1,1536,1536]{1,2,0:T(8,128)(2,1)} async-done(((bf16[1,1536,96]{1,2,0:T(8,128)(2,1)}), bf16[1,1536,1536]{1,2,0:T(8,128)(2,1)}) %all-gather.2.cloned.1.call-update) | async-done | bytes 4718608 | tf_op jit(solution)/shard_map/all_gather | solution.py:50
  89.3 3.8 %fusion.48 = bf16[1536,128]{1,0:T(8,128)(2,1)S(1)} fusion(bf16[128,1536]{1,0:T(8,128)(2,1)S(1)} %copy-done, bf16[1,1536,1536]{1,2,0:T(8,128)(2,1)} %all-gather.2.cloned.1.call-done), kind=kOutput, calls=%fused_computation.47 | convolution fusion | flops 604176384 | bytes 5505024 | tf_op jit(solution)/shard_map/vtc,kc->vtk/dot_general | solution.py:51
  93.1 89.3 %while.15 = (s32[]{:T(128)}, f32[2,4608,1,128]{1,3,2,0:T(8,128)}, bf16[4,384,1,128]{3,1,2,0:T(8,128)(2,1)}, bf16[4,384,1,128]{3,1,2,0:T(8,128)(2,1)}, bf16[4,384...) while((s32[]{:T(128)}, f32[2,4608,1,128]{1,3,2,0:T(8,128)}, ...), condition=%wide.region_4.5_spmd.clone, body=%wide.region_1.4_spmd.clone.sunk | while | flops 2743024640 | bytes 131851096 | solution.py:95
  93.2 2.2 fusion.92
  95.4 1.1 fusion.93
  96.5 1.5 fusion.94
  98.0 2.3 convolution_bitcast_fusion.4
  100.3 1.2 fusion.95
  101.5 1.1 fusion.96
  102.6 1.8 copy-done.1
  104.4 1.7 convolution_bitcast_fusion.5
  106.1 4.6 %maximum_add_fusion.2 = f32[2,4608,1,128]{1,3,2,0:T(8,128)} fusion(f32[1,4608,1,128]{1,3,2,0:T(8,128)} %convolution_bitcast_fusion.4, f32[1,4608,1,128]{1,3,2,0:T(8,128)S(1)} %convolution_bitcast_fusion.5, f32[2,4608,1,128]{1,3,2,0:T(8,128)} %get-tuple-element.258, pred[]{:T(512)S(6)} %compare.7), kind=kLoop, calls=%fused_computation.10.clone.1 | loop fusion | flops 3538944 | bytes 14155777 | tf_op jit(solution)/shard_map/while/body/eval_jaxpr/add | solution.py:90
  111.3 3.1 fusion.97
  114.5 2.2 fusion.92
  116.7 1.1 fusion.93
  117.8 1.5 fusion.94
  119.3 2.3 convolution_bitcast_fusion.4
  121.6 1.2 fusion.95
  122.8 1.1 fusion.96
  123.9 1.8 copy-done.1
  125.6 1.7 convolution_bitcast_fusion.5
  127.4 6.0 %maximum_add_fusion.2 = f32[2,4608,1,128]{1,3,2,0:T(8,128)} fusion(f32[1,4608,1,128]{1,3,2,0:T(8,128)} %convolution_bitcast_fusion.4, f32[1,4608,1,128]{1,3,2,0:T(8,128)S(1)} %convolution_bitcast_fusion.5, f32[2,4608,1,128]{1,3,2,0:T(8,128)} %get-tuple-element.258, pred[]{:T(512)S(6)} %compare.7), kind=kLoop, calls=%fused_computation.10.clone.1 | loop fusion | flops 3538944 | bytes 14155777 | tf_op jit(solution)/shard_map/while/body/eval_jaxpr/add | solution.py:90
  134.0 3.1 fusion.97
  137.2 2.2 fusion.92
  139.4 1.1 fusion.93
  140.5 1.5 fusion.94
  142.0 2.3 convolution_bitcast_fusion.4
  144.3 1.2 fusion.95
  145.5 1.1 fusion.96
  146.6 1.8 copy-done.1
  148.3 1.7 convolution_bitcast_fusion.5
  150.0 6.0 %maximum_add_fusion.2 = f32[2,4608,1,128]{1,3,2,0:T(8,128)} fusion(f32[1,4608,1,128]{1,3,2,0:T(8,128)} %convolution_bitcast_fusion.4, f32[1,4608,1,128]{1,3,2,0:T(8,128)S(1)} %convolution_bitcast_fusion.5, f32[2,4608,1,128]{1,3,2,0:T(8,128)} %get-tuple-element.258, pred[]{:T(512)S(6)} %compare.7), kind=kLoop, calls=%fused_computation.10.clone.1 | loop fusion | flops 3538944 | bytes 14155777 | tf_op jit(solution)/shard_map/while/body/eval_jaxpr/add | solution.py:90
  156.7 3.1 fusion.97
  159.8 2.2 fusion.92
  162.1 1.1 fusion.93
  163.2 1.5 fusion.94
  164.7 2.3 convolution_bitcast_fusion.4
  166.9 1.2 fusion.95
  168.1 1.1 fusion.96
  169.2 1.8 copy-done.1
  171.0 1.7 convolution_bitcast_fusion.5
  172.7 6.0 %maximum_add_fusion.2 = f32[2,4608,1,128]{1,3,2,0:T(8,128)} fusion(f32[1,4608,1,128]{1,3,2,0:T(8,128)} %convolution_bitcast_fusion.4, f32[1,4608,1,128]{1,3,2,0:T(8,128)S(1)} %convolution_bitcast_fusion.5, f32[2,4608,1,128]{1,3,2,0:T(8,128)} %get-tuple-element.258, pred[]{:T(512)S(6)} %compare.7), kind=kLoop, calls=%fused_computation.10.clone.1 | loop fusion | flops 3538944 | bytes 14155777 | tf_op jit(solution)/shard_map/while/body/eval_jaxpr/add | solution.py:90
  179.3 3.1 fusion.97
  182.4 4.2 %fusion.54 = bf16[1536,128]{0,1:T(8,128)(2,1)S(1)} fusion(bf16[1536,128]{1,0:T(8,128)(2,1)} %bitcast.154, bf16[1,1536,1536]{1,2,0:T(8,128)(2,1)} %all-gather.2.cloned.1.call-done), kind=kOutput, calls=%fused_computation.50 | convolution fusion | flops 604176384 | bytes 5505024 | tf_op jit(solution)/shard_map/vtc,vtk->ck/dot_general | solution.py:121
  186.6 0.9 copy.44
  187.8 3.6 %fusion.43 = bf16[1,1536,1536]{2,1,0:T(8,128)(2,1)} fusion(bf16[1536,128]{1,0:T(8,128)(2,1)S(1)} %bitcast.155, bf16[128,1536]{1,0:T(8,128)(2,1)S(1)} %copy-done), kind=kOutput, calls=%fused_computation.41 | convolution fusion | flops 606339072 | bytes 5505024 | tf_op jit(solution)/shard_map/vtk,kc->vtc/dot_general | solution.py:113
  191.4 23.1 %copy.42 = bf16[1,1536,1536]{1,0,2:T(2,128)(2,1)} copy(bf16[1,1536,1536]{2,1,0:T(8,128)(2,1)} %fusion.43) | data formatting | bytes 9437184
  214.5 7.2 %copy.50 = bf16[1536,1,1536]{2,0,1:T(8,128)(2,1)} copy(bf16[1536,1,1536]{2,1,0:T(2,128)(2,1)} %bitcast.150) | data formatting | bytes 9437184
  221.7 6.1 %copy.34 = f32[2,4608,1,128]{3,1,0,2:T(8,128)} copy(f32[2,4608,1,128]{1,3,2,0:T(8,128)} %get-tuple-element.56) | data formatting | bytes 9437184 | tf_op jit(solution)/shard_map/while | solution.py:95
  227.8 2.7 bitcast_convert_fusion
  230.6 1.3 collective-permute-start.3
  231.9 1.3 collective-permute-start.2
  233.2 26.6 %reduce-scatter.9.cloned.1.call-done = bf16[96,128]{1,0:T(8,128)(2,1)} async-done(((bf16[1536,128]{1,0:T(8,128)(2,1)}), bf16[96,128]{1,0:T(8,128)(2,1)}) %reduce-scatter.9.cloned.1.call-update) | async-done | bytes 24592
  259.8 1.5 copy.45
  261.3 1.4 convert_bitcast_fusion
  262.7 1.5 copy.36
  264.2 1.6 fusion.57
  267.4 76.4 %reduce-scatter.7.cloned.1.call-done = bf16[96,1536]{1,0:T(8,128)(2,1)} async-done(((bf16[1536,1536]{1,0:T(8,128)(2,1)}), bf16[96,1536]{1,0:T(8,128)(2,1)}) %reduce-scatter.7.cloned.1.call-update) | async-done | bytes 294928
  343.8 1.3 reshape_bitcast_fusion
  (80 shorter events, 7.3 us)
Async XLA Ops:
  7.2 82.1 %copy-start = (bf16[128,1536]{1,0:T(8,128)(2,1)S(1)}, bf16[128,1536]{1,0:T(8,128)(2,1)}, u32[]{:S(2)}) copy-start(bf16[128,1536]{1,0:T(8,128)(2,1)} %param.12) | copy-start | bytes 1179652
  7.2 82.1 %all-gather.2.cloned.1.call-start = ((), (), s32[]{:S(2)}) async-start(), calls=%async_computation.2 | async-start | bytes 5013504 | tf_op jit(solution)/shard_map/all_gather | solution.py:50
  7.9 251.9 %reduce-scatter.9.cloned.1.call-start = ((), (), s32[]{:S(2)}) async-start(), calls=%async_computation.4 | async-start | bytes 417792
  9.2 5.7 %collective-permute-start.1 = (bf16[2,1,1536,128]{3,2,1,0:T(8,128)(2,1)S(1)}, bf16[2,1,1536,128]{3,2,1,0:T(8,128)(2,1)S(1)}, u32[]{:S(2)}, u32[]{:S(2)}) collective-permute-start(bf16[2,1,1536,128]{3,2,1,0:T(8,128)(2,1)S(1)} %pad_maximum_fusion.1), channel_id=1, source_target_pairs={{1,0},{2,1},{3,2},{4,3},{5,4},{6,5},{7,6},{8,7},{9,8},{10,9},{11,1... | collective-permute-start | bytes 2359304 | tf_op jit(solution)/shard_map/ppermute | solution.py:20
  10.5 4.9 %collective-permute-start = (bf16[2,1,1536,128]{3,2,1,0:T(8,128)(2,1)S(1)}, bf16[2,1,1536,128]{3,2,1,0:T(8,128)(2,1)S(1)}, u32[]{:S(2)}, u32[]{:S(2)}) collective-permute-start(bf16[2,1,1536,128]{3,2,1,0:T(8,128)(2,1)S(1)} %pad_maximum_fusion.1), channel_id=1, source_target_pairs={{0,1},{1,2},{2,3},{3,4},{4,5},{5,6},{6,7},{7,8},{8,9},{9,10},{10,1... | collective-permute-start | bytes 2359304 | tf_op jit(solution)/shard_map/ppermute | solution.py:18
  93.1 2.3 copy-start.5
  93.1 8.4 %copy-start.3 = (bf16[4608,1,128]{2,0,1:T(8,128)(2,1)}, bf16[4608,1,128]{2,0,1:T(8,128)(2,1)S(1)}, u32[]{:S(2)}) copy-start(bf16[4608,1,128]{2,0,1:T(8,128)(2,1)S(1)} %get-tuple-element.276) | copy-start | bytes 3538948 | tf_op jit(solution)/shard_map/while
  102.6 1.8 copy-start.1
  106.1 5.3 %copy-start.2 = (bf16[384,4608]{1,0:T(8,128)(2,1)S(1)}, bf16[384,4608]{1,0:T(8,128)(2,1)}, u32[]{:S(2)}) copy-start(bf16[384,4608]{1,0:T(8,128)(2,1)} %copy-done.1) | copy-start | bytes 10616836 | tf_op jit(solution)/shard_map/while
  110.7 3.7 %copy-start.4 = (bf16[4608,1,128]{2,0,1:T(8,128)(2,1)S(1)}, bf16[4608,1,128]{2,0,1:T(8,128)(2,1)}, u32[]{:S(2)}) copy-start(bf16[4608,1,128]{2,0,1:T(8,128)(2,1)} %copy-done.3) | copy-start | bytes 3538948 | tf_op jit(solution)/shard_map/while
  110.7 3.7 %copy-start.6 = (bf16[4608,1,128]{2,0,1:T(8,128)(2,1)S(1)}, bf16[4608,1,128]{2,0,1:T(8,128)(2,1)}, u32[]{:S(2)}) copy-start(bf16[4608,1,128]{2,0,1:T(8,128)(2,1)} %copy-done.5) | copy-start | bytes 3538948 | tf_op jit(solution)/shard_map/while
  114.4 2.3 copy-start.5
  114.4 8.4 %copy-start.3 = (bf16[4608,1,128]{2,0,1:T(8,128)(2,1)}, bf16[4608,1,128]{2,0,1:T(8,128)(2,1)S(1)}, u32[]{:S(2)}) copy-start(bf16[4608,1,128]{2,0,1:T(8,128)(2,1)S(1)} %get-tuple-element.276) | copy-start | bytes 3538948 | tf_op jit(solution)/shard_map/while
  123.9 1.8 copy-start.1
  127.3 6.6 %copy-start.2 = (bf16[384,4608]{1,0:T(8,128)(2,1)S(1)}, bf16[384,4608]{1,0:T(8,128)(2,1)}, u32[]{:S(2)}) copy-start(bf16[384,4608]{1,0:T(8,128)(2,1)} %copy-done.1) | copy-start | bytes 10616836 | tf_op jit(solution)/shard_map/while
  133.3 3.7 %copy-start.4 = (bf16[4608,1,128]{2,0,1:T(8,128)(2,1)S(1)}, bf16[4608,1,128]{2,0,1:T(8,128)(2,1)}, u32[]{:S(2)}) copy-start(bf16[4608,1,128]{2,0,1:T(8,128)(2,1)} %copy-done.3) | copy-start | bytes 3538948 | tf_op jit(solution)/shard_map/while
  133.3 3.7 %copy-start.6 = (bf16[4608,1,128]{2,0,1:T(8,128)(2,1)S(1)}, bf16[4608,1,128]{2,0,1:T(8,128)(2,1)}, u32[]{:S(2)}) copy-start(bf16[4608,1,128]{2,0,1:T(8,128)(2,1)} %copy-done.5) | copy-start | bytes 3538948 | tf_op jit(solution)/shard_map/while
  137.1 2.3 copy-start.5
  137.1 8.4 %copy-start.3 = (bf16[4608,1,128]{2,0,1:T(8,128)(2,1)}, bf16[4608,1,128]{2,0,1:T(8,128)(2,1)S(1)}, u32[]{:S(2)}) copy-start(bf16[4608,1,128]{2,0,1:T(8,128)(2,1)S(1)} %get-tuple-element.276) | copy-start | bytes 3538948 | tf_op jit(solution)/shard_map/while
  146.6 1.8 copy-start.1
  150.0 6.6 %copy-start.2 = (bf16[384,4608]{1,0:T(8,128)(2,1)S(1)}, bf16[384,4608]{1,0:T(8,128)(2,1)}, u32[]{:S(2)}) copy-start(bf16[384,4608]{1,0:T(8,128)(2,1)} %copy-done.1) | copy-start | bytes 10616836 | tf_op jit(solution)/shard_map/while
  156.0 3.7 %copy-start.4 = (bf16[4608,1,128]{2,0,1:T(8,128)(2,1)S(1)}, bf16[4608,1,128]{2,0,1:T(8,128)(2,1)}, u32[]{:S(2)}) copy-start(bf16[4608,1,128]{2,0,1:T(8,128)(2,1)} %copy-done.3) | copy-start | bytes 3538948 | tf_op jit(solution)/shard_map/while
  156.0 3.7 %copy-start.6 = (bf16[4608,1,128]{2,0,1:T(8,128)(2,1)S(1)}, bf16[4608,1,128]{2,0,1:T(8,128)(2,1)}, u32[]{:S(2)}) copy-start(bf16[4608,1,128]{2,0,1:T(8,128)(2,1)} %copy-done.5) | copy-start | bytes 3538948 | tf_op jit(solution)/shard_map/while
  159.8 2.3 copy-start.5
  159.8 8.3 %copy-start.3 = (bf16[4608,1,128]{2,0,1:T(8,128)(2,1)}, bf16[4608,1,128]{2,0,1:T(8,128)(2,1)S(1)}, u32[]{:S(2)}) copy-start(bf16[4608,1,128]{2,0,1:T(8,128)(2,1)S(1)} %get-tuple-element.276) | copy-start | bytes 3538948 | tf_op jit(solution)/shard_map/while
  169.2 1.8 copy-start.1
  172.7 6.6 %copy-start.2 = (bf16[384,4608]{1,0:T(8,128)(2,1)S(1)}, bf16[384,4608]{1,0:T(8,128)(2,1)}, u32[]{:S(2)}) copy-start(bf16[384,4608]{1,0:T(8,128)(2,1)} %copy-done.1) | copy-start | bytes 10616836 | tf_op jit(solution)/shard_map/while
  178.7 3.7 %copy-start.4 = (bf16[4608,1,128]{2,0,1:T(8,128)(2,1)S(1)}, bf16[4608,1,128]{2,0,1:T(8,128)(2,1)}, u32[]{:S(2)}) copy-start(bf16[4608,1,128]{2,0,1:T(8,128)(2,1)} %copy-done.3) | copy-start | bytes 3538948 | tf_op jit(solution)/shard_map/while
  178.7 3.7 %copy-start.6 = (bf16[4608,1,128]{2,0,1:T(8,128)(2,1)S(1)}, bf16[4608,1,128]{2,0,1:T(8,128)(2,1)}, u32[]{:S(2)}) copy-start(bf16[4608,1,128]{2,0,1:T(8,128)(2,1)} %copy-done.5) | copy-start | bytes 3538948 | tf_op jit(solution)/shard_map/while
  182.4 5.4 %copy-start.7 = (bf16[4,384,1,128]{3,1,2,0:T(8,128)(2,1)S(1)}, bf16[4,384,1,128]{3,1,2,0:T(8,128)(2,1)}, u32[]{:S(2)}) copy-start(bf16[4,384,1,128]{3,1,2,0:T(8,128)(2,1)} %get-tuple-element.54) | copy-start | bytes 1179652
  187.6 156.3 %reduce-scatter.7.cloned.1.call-start = ((), (), s32[]{:S(2)}) async-start(), calls=%async_computation.3 | async-start | bytes 5013504
  230.6 33.6 %collective-permute-start.3 = (bf16[1,2,1536,128]{3,2,1,0:T(8,128)(2,1)S(1)}, bf16[1,2,1536,128]{3,2,1,0:T(8,128)(2,1)S(1)}, u32[]{:S(2)}, u32[]{:S(2)}) collective-permute-start(bf16[1,2,1536,128]{3,2,1,0:T(8,128)(2,1)S(1)} %get-tuple-element.180), channel_id=1, source_target_pairs={{0,1},{1,2},{2,3},{3,4},{4,5},{5,6},{6,7},{7,8},{8,9},{9,10},{10,1... | collective-permute-start | bytes 2359304 | tf_op jit(solution)/shard_map/ppermute | solution.py:30
  231.9 32.3 %collective-permute-start.2 = (bf16[1,2,1536,128]{3,2,1,0:T(8,128)(2,1)S(1)}, bf16[1,2,1536,128]{3,2,1,0:T(8,128)(2,1)S(1)}, u32[]{:S(2)}, u32[]{:S(2)}) collective-permute-start(bf16[1,2,1536,128]{3,2,1,0:T(8,128)(2,1)S(1)} %get-tuple-element.179), channel_id=1, source_target_pairs={{1,0},{2,1},{3,2},{4,3},{5,4},{6,5},{7,6},{8,7},{9,8},{10,9},{11,1... | collective-permute-start | bytes 2359304 | tf_op jit(solution)/shard_map/ppermute | solution.py:30
Sparse Core Ops, SparseCore 0:
  9.8 79.4 all-gather.1
  187.7 72.0 reduce-scatter.8
  262.6 81.1 reduce-scatter.6
where the time goes:
time: 354 us; the launch traced here: 352 us
  waiting for transfers between devices  177 us (50%)
  matrix products  57.8 us (16%)
  local copies, waits for them, and re-layouts  53.6 us (15%)
  other arithmetic  42.8 us (12%)
  between operations  13.9 us (4%)
  starting transfers between devices  7.3 us (2%)
    unnamed x5, waiting for transfers between devices  104 us
    all_gather x1, waiting for transfers between devices, body(): grad_full = lax.all_gather(out_grad, 'fsdp', axis=2, tiled=True)  72.5 us
    unnamed x13, local copies, waits for them, and re-layouts  36.3 us
    add x4, other arithmetic, one_tile(): carry + jnp.stack((key_part, value_part))  22.5 us
    dot_general x4, matrix products, one_tile(): jnp.einsum('hik,khd->ihd', score_grad, key_band, preferred_element_type=j...  12.3 us
    dot_general x4, matrix products, one_tile(): jnp.einsum('hik,ihd->khd', weights, back_tile, preferred_element_type=jnp...  9.18 us
    dot_general x4, matrix products, one_tile(): jnp.einsum('ihd,khd->hik', query_tile, key_band, preferred_element_type=j...  8.94 us
    while x48, local copies, waits for them, and re-layouts  7.11 us
  transfers between devices with their start and end apart: 7, of which 4 were waited for; matrix products, arithmetic and copies ran while one was open for 15% of the time, Pallas kernels for 0%

commit v1 on v0

v1 whole, which is shorter than its diff:
```python
import functools

import jax
import jax.numpy as jnp
from jax import lax
from jax.experimental import pallas as pl
from jax.experimental.pallas import tpu as pltpu
from jax.sharding import Mesh
from jax.sharding import PartitionSpec as P

HDIM = 128
TILE = 384
TF = 2
TC = 2
ROW_TILES = TF * TC
BAND = 3 * ROW_TILES
SCALING = HDIM ** (-0.5)
LOG2E = 1.4426950408889634
BF = jnp.bfloat16
F32 = jnp.float32
ST = ("y", "xh", "core")
NT = (((1,), (1,)), ((), ()))
TN = (((0,), (0,)), ((), ()))
NN = (((1,), (0,)), ((), ()))


def dot(a, b, dims):
    return lax.dot_general(a, b, dims, preferred_element_type=F32)


def build_list(pattern_ref, list_ref, tile):
    frame, col = tile // TC, tile % TC
    count = jnp.int32(0)
    for place in range(BAND):
        row, key_frame, key_col = place // ROW_TILES, place // TC % TF, place % TC
        slot = (key_frame - frame + 1) * 9 + row * 3 + (key_col - col + 1)
        list_ref[tile, count] = jnp.int32(place)
        count = count + (pattern_ref[tile, slot] >= 0).astype(jnp.int32)
    return count


def fill_band(refs, band, sem):
    copies = [
        pltpu.make_async_copy(ref, band.at[pl.ds(i * ROW_TILES, ROW_TILES)], sem.at[i])
        for i, ref in enumerate(refs)
    ]
    for copy in copies:
        copy.start()
    return copies


def forward_kernel(
    pattern_ref, q_ref, ka_ref, ko_ref, kb_ref, va_ref, vo_ref, vb_ref,
    att_ref, lse_ref,
    kband, vband, list_ref, top, total, acc, ksem, vsem,
):
    copies = fill_band((ka_ref, ko_ref, kb_ref), kband, ksem)
    copies += fill_band((va_ref, vo_ref, vb_ref), vband, vsem)
    counts = [build_list(pattern_ref, list_ref, t) for t in range(ROW_TILES)]
    for copy in copies:
        copy.wait()
    for tile in range(ROW_TILES):
        top[...] = jnp.full(top.shape, -jnp.inf, F32)
        total[...] = jnp.zeros(total.shape, F32)
        acc[...] = jnp.zeros(acc.shape, F32)

        def step(i, carry):
            place = list_ref[tile, i]
            scores = dot(q_ref[tile], kband[place], NT) * (SCALING * LOG2E)
            before = top[...]
            peak = jnp.maximum(before, jnp.max(scores, axis=1, keepdims=True))
            raised = jnp.exp2(scores - peak)
            shrink = jnp.exp2(before - peak)
            top[...] = peak
            total[...] = shrink * total[...] + jnp.sum(raised, axis=1, keepdims=True)
            acc[...] = shrink * acc[...] + dot(raised.astype(BF), vband[place], NN)
            return carry

        lax.fori_loop(0, counts[tile], step, 0)
        att_ref[tile] = (acc[...] / total[...]).astype(BF)
        lse = top[...] + jnp.log2(total[...])
        lse_ref[tile] = jnp.broadcast_to(lse, (TILE, HDIM)).T[:8]


def backward_kernel(
    pattern_ref, q_ref, ka_ref, ko_ref, kb_ref, va_ref, vo_ref, vb_ref,
    back_ref, att_ref, lse_ref,
    dq_ref, up_ref, down_ref, own_ref,
    kband, vband, list_ref, dk, dv, dq, ksem, vsem,
):
    copies = fill_band((ka_ref, ko_ref, kb_ref), kband, ksem)
    copies += fill_band((va_ref, vo_ref, vb_ref), vband, vsem)
    counts = [build_list(pattern_ref, list_ref, t) for t in range(ROW_TILES)]
    dk[...] = jnp.zeros(dk.shape, F32)
    dv[...] = jnp.zeros(dv.shape, F32)
    for copy in copies:
        copy.wait()
    for tile in range(ROW_TILES):
        dq[...] = jnp.zeros(dq.shape, F32)
        prod = back_ref[tile].astype(F32) * att_ref[tile].astype(F32)
        delta = jnp.sum(prod.T, axis=0, keepdims=True)
        lse = lse_ref[tile][:1]

        def step(i, carry):
            place = list_ref[tile, i]
            queries, back = q_ref[tile], back_ref[tile]
            keys, values = kband[place], vband[place]
            scores = dot(keys, queries, NT) * (SCALING * LOG2E)
            prob = jnp.exp2(scores - lse)
            dv[place] += dot(prob.astype(BF), back, NN)
            prob_grad = dot(values, back, NT)
            score_grad = (prob * (prob_grad - delta)).astype(BF)
            dk[place] += dot(score_grad, queries, NN)
            dq[...] += dot(score_grad, keys, TN)
            return carry

        lax.fori_loop(0, counts[tile], step, 0)
        dq_ref[tile] = (dq[...] * SCALING).astype(BF)
    for i in range(ROW_TILES):
        up_ref[0, i] = dk[i].astype(BF)
        up_ref[1, i] = dv[i].astype(BF)
        down_ref[0, i] = dk[2 * ROW_TILES + i].astype(BF)
        down_ref[1, i] = dv[2 * ROW_TILES + i].astype(BF)
        own_ref[0, i] = dk[ROW_TILES + i]
        own_ref[1, i] = dv[ROW_TILES + i]


VMEM_SPEC = pl.BlockSpec(memory_space=pltpu.VMEM)
SMEM_SPEC = pl.BlockSpec(memory_space=pltpu.SMEM)
ANY_SPEC = pl.BlockSpec(memory_space=pl.ANY)
BLOCK = (ROW_TILES, TILE, HDIM)
BAND_SCRATCH = [
    pltpu.VMEM((BAND, TILE, HDIM), BF),
    pltpu.VMEM((BAND, TILE, HDIM), BF),
    pltpu.SMEM((ROW_TILES, BAND + 1), jnp.int32),
]
PARAMS = pltpu.CompilerParams(vmem_limit_bytes=40 * 1024 * 1024)


def forward(pattern, queries, band):
    return pl.pallas_call(
        forward_kernel,
        name="attention_forward",
        out_shape=(
            jax.ShapeDtypeStruct(BLOCK, BF),
            jax.ShapeDtypeStruct((ROW_TILES, 8, TILE), F32),
        ),
        in_specs=[SMEM_SPEC, VMEM_SPEC] + [ANY_SPEC] * 6,
        out_specs=(VMEM_SPEC, VMEM_SPEC),
        scratch_shapes=BAND_SCRATCH
        + [
            pltpu.VMEM((TILE, 1), F32),
            pltpu.VMEM((TILE, 1), F32),
            pltpu.VMEM((TILE, HDIM), F32),
            pltpu.SemaphoreType.DMA((3,)),
            pltpu.SemaphoreType.DMA((3,)),
        ],
        compiler_params=PARAMS,
        cost_estimate=pl.CostEstimate(
            flops=3_000_000_000, bytes_accessed=4_000_000, transcendentals=7_000_000
        ),
    )(pattern, queries, *band)


def backward(pattern, queries, band, back, attended, lse):
    return pl.pallas_call(
        backward_kernel,
        name="attention_backward",
        out_shape=(
            jax.ShapeDtypeStruct(BLOCK, BF),
            jax.ShapeDtypeStruct((2,) + BLOCK, BF),
            jax.ShapeDtypeStruct((2,) + BLOCK, BF),
            jax.ShapeDtypeStruct((2,) + BLOCK, F32),
        ),
        in_specs=[SMEM_SPEC, VMEM_SPEC] + [ANY_SPEC] * 6 + [VMEM_SPEC] * 3,
        out_specs=(VMEM_SPEC,) * 4,
        scratch_shapes=BAND_SCRATCH
        + [
            pltpu.VMEM((BAND, TILE, HDIM), F32),
            pltpu.VMEM((BAND, TILE, HDIM), F32),
            pltpu.VMEM((TILE, HDIM), F32),
            pltpu.SemaphoreType.DMA((3,)),
            pltpu.SemaphoreType.DMA((3,)),
        ],
        compiler_params=PARAMS,
        cost_estimate=pl.CostEstimate(
            flops=8_000_000_000, bytes_accessed=8_000_000, transcendentals=7_000_000
        ),
    )(pattern, queries, *band, back, attended, lse)


def shifted(block, distance):
    route = [(i - distance, i) for i in range(16) if 0 <= i - distance < 16]
    return lax.ppermute(block, ST, route)


def swapped(block):
    return lax.ppermute(block, "xl", [(0, 1), (1, 0)])


def body(queries, key_rows, value_rows, out_grad, proj_weight, pattern):
    half = lax.axis_index("xl")
    tokens = queries.shape[1]
    q = queries.reshape(BLOCK)
    kv = jnp.stack((key_rows.reshape(BLOCK), value_rows.reshape(BLOCK)))
    above, below = shifted(kv, 1), shifted(kv, -1)
    band = (above[0], kv[0], below[0], above[1], kv[1], below[1])

    grad_half = lax.all_gather(out_grad[0].T, "z", axis=0, tiled=True)
    feats = grad_half.shape[0]
    w_mine = lax.dynamic_slice_in_dim(proj_weight, half * feats, feats, 1)
    w_other = swapped(lax.dynamic_slice_in_dim(proj_weight, (1 - half) * feats, feats, 1))

    attended, lse = forward(pattern, q, band)
    att = attended.reshape(tokens, HDIM)
    att_other = swapped(att)

    back_other = lax.dot_general(grad_half, w_other, (((0,), (1,)), ((), ())),
                                 preferred_element_type=F32).astype(BF)
    back_got = swapped(back_other)
    back_mine = lax.dot_general(grad_half, w_mine, (((0,), (1,)), ((), ())),
                                preferred_element_type=F32)
    back = (back_mine + back_got.astype(F32)).astype(BF)

    part = lax.dot_general(w_mine, att, (((0,), (1,)), ((), ())), preferred_element_type=F32)
    part = part + lax.dot_general(
        w_other, att_other, (((0,), (1,)), ((), ())), preferred_element_type=F32
    )
    projected = lax.psum_scatter(part.astype(BF), "z", scatter_dimension=0, tiled=True)
    projected = projected.T[None]

    wg_mine = dot(grad_half, att, NN).astype(BF)
    wg_other = dot(grad_half, att_other, NN).astype(BF)
    first = jnp.where(half == 0, wg_mine, wg_other)
    second = jnp.where(half == 0, wg_other, wg_mine)
    pieces = jnp.stack((first, second)).reshape(16, 96, HDIM)
    pieces = lax.all_to_all(pieces, ST, 0, 0, tiled=True)
    summed = jnp.sum(pieces.astype(F32), axis=0)
    route = [
        (h * 4 + 2 * a + y, a * 4 + 2 * h + y)
        for h in range(2)
        for a in range(2)
        for y in range(2)
    ]
    weight_grad = lax.ppermute(summed, ("xl", "y"), route).T

    dq, up, down, own = backward(
        pattern, q, band, back.reshape(BLOCK), attended, lse
    )
    total = own + shifted(up, -1).astype(F32) + shifted(down, 1).astype(F32)
    shape = (1, tokens, HDIM)
    key_grad = (SCALING * total[0]).astype(BF).reshape(shape)
    value_grad = total[1].astype(BF).reshape(shape)
    return projected, dq.reshape(shape), key_grad, value_grad, weight_grad


def solution(mesh):
    fine = Mesh(mesh.devices.reshape(2, 8, 4, 2, 2), ("xl", "z", "y", "xh", "core"))
    fsdp = ("xl", "z")
    rows = P(None, ST, fsdp)
    return jax.shard_map(
        body,
        mesh=fine,
        in_specs=(rows, rows, rows, rows, P(fsdp, None), P(ST, None)),
        out_specs=(rows, rows, rows, rows, P(fsdp, ST)),
        check_vma=False,
    )
```

time: 354 us -> 174 us (0.49)
  waiting for transfers between devices: 177 us -> 26.9 us
  matrix products: 57.8 us -> 8.33 us
  local copies, waits for them, and re-layouts: 53.6 us -> 9.55 us
  Pallas kernels: 0 us -> 39.1 us
  other arithmetic: 42.8 us -> 3.94 us
  blocking collectives: 0 us -> 30.8 us
  starting transfers between devices: 7.3 us -> 38 us
    unnamed x5 -> x2, waiting for transfers between devices: 104 us -> 0.7 us
    all_gather x1, waiting for transfers between devices: 72.5 us -> 5.61 us  [body(): grad_half = lax.all_gather(out_grad[0].T, 'z', axis=0, tiled=True)]
    dot_general x27 -> x6, matrix products: 57.8 us -> 8.33 us  [the longest x2 2.52 us: dot(): return lax.dot_general(a, b, dims, preferred_element_type=F32)]
    pallas_call x0 -> x2, Pallas kernels: none -> 39.1 us  [the longest x1 20.1 us: forward(): pl.pallas_call(forward_kernel, name='attention_forward', out_shape=(jax.S...]
    ppermute x4 -> x8, starting transfers between devices: 7 us -> 38 us  [the longest x4 31.7 us: shifted(): return lax.ppermute(block, ST, route)]
    all_to_all x0 -> x1, blocking collectives: none -> 30.8 us  [body(): pieces = lax.all_to_all(pieces, ST, 0, 0, tiled=True)]
    unnamed x13 -> x43, local copies, waits for them, and re-layouts: 36.3 us -> 7.08 us
    add x6 -> x1, other arithmetic: 24.2 us -> 1.65 us  [body(): total = own + shifted(up, -1).astype(F32) + shifted(down, 1).astype(F32)]
  transfers between devices with their start and end apart: 7 -> 10, of which waited for: 4 -> 5; matrix products, arithmetic and copies ran while one was open for 15% -> 9% of each run, Pallas kernels for 0% -> 23%
where the time goes in v1:
time: 174 us; the launch traced here: 171 us
  Pallas kernels  39.1 us (22%)
  starting transfers between devices  38 us (22%)
  blocking collectives  30.8 us (18%)
  waiting for transfers between devices  26.9 us (15%)
  between operations  14.4 us (8%)
  local copies, waits for them, and re-layouts  9.55 us (5%)
  matrix products  8.33 us (5%)
  other arithmetic  3.94 us (2%)
    ppermute x4, starting transfers between devices, shifted(): return lax.ppermute(block, ST, route)  31.7 us
    all_to_all x1, blocking collectives, body(): pieces = lax.all_to_all(pieces, ST, 0, 0, tiled=True)  30.8 us
    pallas_call x1, Pallas kernels, forward(): pl.pallas_call(forward_kernel, name='attention_forward', out_shape=(jax.S...  20.1 us
    pallas_call x1, Pallas kernels, backward(): pl.pallas_call(backward_kernel, name='attention_backward', out_shape=(jax...  19.1 us
    ppermute x3, waiting for transfers between devices, swapped(): return lax.ppermute(block, 'xl', [(0, 1), (1, 0)])  14.9 us
    unnamed x43, local copies, waits for them, and re-layouts  7.08 us
    all_gather x1, waiting for transfers between devices, body(): grad_half = lax.all_gather(out_grad[0].T, 'z', axis=0, tiled=True)  5.61 us
    ppermute x1, waiting for transfers between devices, body(): weight_grad = lax.ppermute(summed, ('xl', 'y'), route).T  5.03 us
  transfers between devices with their start and end apart: 10, of which 5 were waited for; matrix products, arithmetic and copies ran while one was open for 9% of the time, Pallas kernels for 23%

profile of v1, /device:TPU:2, one launch (start us, length us, event | category | flops | bytes accessed | tf_op | source)
XLA Modules:
  0.0 171.0 jit_solution(9487450157949331257)
XLA Ops:
  7.2 0.0 copy-start
  7.2 0.0 all-gather.2.cloned.1.call-start
  7.2 0.7 all-gather.2.cloned.1.call-update
  7.9 0.0 reduce-scatter.2.cloned.1.call-start
  8.0 0.0 copy-start.1
  8.0 0.0 copy-start.2
  8.0 0.0 copy-start.11
  8.0 0.0 copy-start.13
  8.0 1.3 pad_maximum_fusion
  9.3 1.3 collective-permute-start.1
  10.6 3.1 %collective-permute-start = (bf16[2,4,384,128]{3,2,1,0:T(8,128)(2,1)S(1)}, bf16[2,4,384,128]{3,2,1,0:T(8,128)(2,1)S(1)}, u32[]{:S(2)}, u32[]{:S(2)}) collective-permute-start(bf16[2,4,384,128]{3,2,1,0:T(8,128)(2,1)S(1)} %pad_maximum_fusion), channel_id=1, source_target_pairs={{0,1},{1,2},{2,3},{3,4},{4,5},{5,6},{6,7},{7,8},{8,9},{9,10},{10,1... | collective-permute-start | bytes 2359304 | tf_op jit(solution)/shard_map/ppermute | solution.py:194
  13.7 0.0 collective-permute-done.1
  13.7 1.2 slice_bitcast_fusion
  14.9 0.0 copy-start.3
  14.9 0.0 copy-start.5
  14.9 0.6 collective-permute-done
  15.5 0.1 slice_bitcast_fusion.1
  15.6 0.0 copy-start.7
  15.6 0.0 copy-start.9
  15.6 0.0 copy-done.1
  15.6 0.0 copy-done.2
  15.6 20.1 %attention_forward.1 = (bf16[4,384,128]{2,1,0:T(8,128)(2,1)S(1)}, f32[4,8,384]{2,1,0:T(8,128)S(1)}) custom-call(s32[4,27]{1,0:T(4,128)S(1)} %copy-done.13, bf16[4,384,128]{2,1,0:T(8,128)(2,1)S(1)} %bitcast.58, bf16[4,384,128]{2,1,0:T(8,128)(2,1)S(1)} %get-tuple-element.20.ka_ref, bf16[4,384,128]{2,1,0:T(8,128)(2,1)S(1)} %bitcast.56, ...), custom_call_target="tpu_custom_call" | custom-call | flops 3000000000 | bytes 4000000 | tf_op jit(solution)/shard_map/attention_forward/pallas_call | solution.py:141
  35.8 0.0 copy-start.14
  35.8 0.6 copy-done.14
  36.4 2.3 %collective-permute-start.3 = (bf16[1536,128]{1,0:T(8,128)(2,1)S(1)}, bf16[1536,128]{1,0:T(8,128)(2,1)S(1)}, u32[]{:S(2)}, u32[]{:S(2)}) collective-permute-start(bf16[1536,128]{1,0:T(8,128)(2,1)S(1)} %bitcast.48), channel_id=1, source_target_pairs={{0,128},{128,0},{1,129},{129,1},{2,130},{130,2},{3,131},{131,3},{4... | collective-permute-start | bytes 1179656 | tf_op jit(solution)/shard_map/ppermute | solution.py:198
  38.7 0.1 collective-permute-start.2
  38.8 0.8 fusion.3
  39.6 6.9 %collective-permute-done.2 = bf16[128,768]{1,0:T(8,128)(2,1)S(1)} collective-permute-done((bf16[128,768]{1,0:T(8,128)(2,1)S(1)}, bf16[128,768]{1,0:T(8,128)(2,1)S(1)}, u32[]{:S(2)}, u32[]{:S(2)}) %collective-permute-start.2) | collective-permute-done | bytes 196640 | tf_op jit(solution)/shard_map/ppermute | solution.py:198
  46.5 0.0 collective-permute-done.3
  46.5 2.2 %add_convert_fusion = bf16[768,1536]{1,0:T(8,128)(2,1)} fusion(f32[768,1536]{1,0:T(8,128)S(1)} %fusion.3, bf16[128,768]{1,0:T(8,128)(2,1)S(1)} %collective-permute-done.2, bf16[1536,128]{1,0:T(8,128)(2,1)S(1)} %collective-permute-done.3), kind=kOutput, calls=%fused_computation | convolution fusion | flops 304349184 | bytes 7667712 | tf_op jit(solution)/shard_map/dot_general | solution.py:226
  48.7 0.0 copy-done.18
  48.8 0.0 reduce-scatter.2.cloned.1.call-update
  48.8 5.6 %all-gather.2.cloned.1.call-done = bf16[768,1536]{1,0:T(8,128)(2,1)} async-done(((bf16[96,1536]{1,0:T(8,128)(2,1)}), bf16[768,1536]{1,0:T(8,128)(2,1)}) %all-gather.2.cloned.1.call-update) | async-done | bytes 2359312 | tf_op jit(solution)/shard_map/all_gather | solution.py:209
  54.4 2.3 %fusion = bf16[1536,128]{0,1:T(8,128)(2,1)S(1)} fusion(bf16[128,768]{1,0:T(8,128)(2,1)S(1)} %collective-permute-done.2, bf16[768,1536]{1,0:T(8,128)(2,1)} %all-gather.2.cloned.1.call-done), kind=kOutput, calls=%fused_computation.3 | convolution fusion | flops 302186496 | bytes 2949120 | tf_op jit(solution)/shard_map/dot_general | solution.py:218
  56.7 0.6 collective-permute-start.4
  57.3 0.0 copy-done.16
  57.3 1.6 convolution_convert_fusion.2
  58.9 0.5 convolution_bitcast_fusion
  59.4 7.9 %collective-permute-done.4 = bf16[1536,128]{0,1:T(8,128)(2,1)S(1)} collective-permute-done((bf16[1536,128]{0,1:T(8,128)(2,1)S(1)}, bf16[1536,128]{0,1:T(8,128)(2,1)S(1)}, u32[]{:S(2)}, u32[]{:S(2)}) %collective-permute-start.4) | collective-permute-done | bytes 393248 | tf_op jit(solution)/shard_map/ppermute | solution.py:198
  67.4 0.1 add_convert_fusion.1
  67.4 0.2 copy.12
  67.7 1.0 copy-done.4
  68.7 1.0 copy-done.6
  69.7 1.0 copy-done.8
  70.7 1.0 copy-done.10
  71.7 1.0 copy-done.12
  72.7 0.8 copy-done.15
  73.5 19.1 %attention_backward.1 = (bf16[4,384,128]{2,1,0:T(8,128)(2,1)}, bf16[2,4,384,128]{3,2,1,0:T(8,128)(2,1)}, bf16[2,4,384,128]{3,2,1,0:T(8,128)(2,1)}, f32[2,4,384,128]{3,2,1,0:T(8,128)S(1)}) custom-call(s32[4,27]{1,0:T(4,128)S(1)} %copy-done.13, bf16[4,384,128]{2,1,0:T(8,128)(2,1)S(1)} %bitcast.59, bf16[4,384,128]{2,1,0:T(8,128)(2,1)S(1)} %copy-done.10, ...), custom_call_target="tpu_custom_call" | custom-call | flops 8000000000 | bytes 8000000 | tf_op jit(solution)/shard_map/attention_backward/pallas_call | solution.py:166
  92.5 1.3 collective-permute-start.5
  93.8 26.0 %collective-permute-start.6 = (bf16[2,4,384,128]{3,2,1,0:T(8,128)(2,1)}, bf16[2,4,384,128]{3,2,1,0:T(8,128)(2,1)}, u32[]{:S(2)}, u32[]{:S(2)}) collective-permute-start(bf16[2,4,384,128]{3,2,1,0:T(8,128)(2,1)} %get-tuple-element.16), channel_id=1, source_target_pairs={{0,1},{1,2},{2,3},{3,4},{4,5},{5,6},{6,7},{7,8},{8,9},{9,10},{10,1... | collective-permute-start | bytes 2359304 | tf_op jit(solution)/shard_map/ppermute | solution.py:194
  119.8 0.0 copy-done.17
  119.8 0.0 copy-done.20
  119.8 0.9 select_bitcast_fusion.1
  120.8 0.2 copy.13
  121.0 30.8 %all_to_all.5 = bf16[16,96,128]{2,1,0:T(8,128)(2,1)S(1)} all-to-all(bf16[16,96,128]{2,1,0:T(8,128)(2,1)S(1)} %bitcast.60), channel_id=1, replica_groups=mesh['xl'=2,'z'=8,'y'=4,'xh'=2,'core'=2] {'y','xh','core'}, dimensions={0} | all-to-all | bytes 786432 | tf_op jit(solution)/shard_map/all_to_all | solution.py:237
  151.8 0.1 convert_reduce_fusion
  151.9 3.3 %collective-permute-start.7 = (f32[96,128]{1,0:T(8,128)S(1)}, f32[96,128]{1,0:T(8,128)S(1)}, u32[]{:S(2)}, u32[]{:S(2)}) collective-permute-start(f32[96,128]{1,0:T(8,128)S(1)} %convert_reduce_fusion), channel_id=1, source_target_pairs={{0,0},{4,4},{8,128},{12,132},{128,8},{132,12},{136,136},{140,140},... | collective-permute-start | bytes 147464 | tf_op jit(solution)/shard_map/ppermute | solution.py:245
  155.2 5.0 %collective-permute-done.7 = f32[96,128]{1,0:T(8,128)S(1)} collective-permute-done((f32[96,128]{1,0:T(8,128)S(1)}, f32[96,128]{1,0:T(8,128)S(1)}, u32[]{:S(2)}, u32[]{:S(2)}) %collective-permute-start.7) | collective-permute-done | bytes 49184 | tf_op jit(solution)/shard_map/ppermute | solution.py:245
  160.3 0.0 collective-permute-done.5
  160.3 0.0 collective-permute-done.6
  160.3 1.6 convert_add_fusion
  161.9 0.8 slice.39
  162.7 0.8 fusion.1
  163.6 0.6 copy.15
  (22 shorter events, 0.1 us)
Async XLA Ops:
  7.2 31.5 %copy-start = (bf16[128,1536]{1,0:T(8,128)(2,1)S(1)}, bf16[128,1536]{1,0:T(8,128)(2,1)}, u32[]{:S(2)}) copy-start(bf16[128,1536]{1,0:T(8,128)(2,1)} %param.10) | copy-start | bytes 1179652
  7.2 47.2 %all-gather.2.cloned.1.call-start = ((), (), s32[]{:S(2)}) async-start(), calls=%async_computation.3 | async-start | bytes 2654208 | tf_op jit(solution)/shard_map/all_gather | solution.py:209
  7.9 155.6 %reduce-scatter.2.cloned.1.call-start = ((), (), s32[]{:S(2)}) async-start(), calls=%async_computation.2 | async-start | bytes 2654208 | tf_op jit(solution)/shard_map/reduce_scatter | solution.py:229
  8.0 7.6 %copy-start.1 = (bf16[1,1536,128]{2,1,0:T(8,128)(2,1)S(1)}, bf16[1,1536,128]{2,1,0:T(8,128)(2,1)}, u32[]{:S(2)}) copy-start(bf16[1,1536,128]{2,1,0:T(8,128)(2,1)} %param.8) | copy-start | bytes 1179652
  8.0 7.6 %copy-start.2 = (bf16[1,1536,128]{2,1,0:T(8,128)(2,1)S(1)}, bf16[1,1536,128]{2,1,0:T(8,128)(2,1)}, u32[]{:S(2)}) copy-start(bf16[1,1536,128]{2,1,0:T(8,128)(2,1)} %param.7) | copy-start | bytes 1179652
  8.0 7.6 %copy-start.11 = (bf16[1,1536,128]{2,1,0:T(8,128)(2,1)S(1)}, bf16[1,1536,128]{2,1,0:T(8,128)(2,1)}, u32[]{:S(2)}) copy-start(bf16[1,1536,128]{2,1,0:T(8,128)(2,1)} %param.6) | copy-start | bytes 1179652
  8.0 7.6 %copy-start.13 = (s32[4,27]{1,0:T(4,128)S(1)}, s32[4,27]{1,0:T(4,128)}, u32[]{:S(2)}) copy-start(s32[4,27]{1,0:T(4,128)} %pattern_ref.3) | copy-start | bytes 1300
  9.3 4.4 %collective-permute-start.1 = (bf16[2,4,384,128]{3,2,1,0:T(8,128)(2,1)S(1)}, bf16[2,4,384,128]{3,2,1,0:T(8,128)(2,1)}, u32[]{:S(2)}, u32[]{:S(2)}) collective-permute-start(bf16[2,4,384,128]{3,2,1,0:T(8,128)(2,1)S(1)} %pad_maximum_fusion), channel_id=1, source_target_pairs={{1,0},{2,1},{3,2},{4,3},{5,4},{6,5},{7,6},{8,7},{9,8},{10,9},{11,1... | collective-permute-start | bytes 2359304 | tf_op jit(solution)/shard_map/ppermute | solution.py:194
  10.6 4.9 %collective-permute-start = (bf16[2,4,384,128]{3,2,1,0:T(8,128)(2,1)S(1)}, bf16[2,4,384,128]{3,2,1,0:T(8,128)(2,1)S(1)}, u32[]{:S(2)}, u32[]{:S(2)}) collective-permute-start(bf16[2,4,384,128]{3,2,1,0:T(8,128)(2,1)S(1)} %pad_maximum_fusion), channel_id=1, source_target_pairs={{0,1},{1,2},{2,3},{3,4},{4,5},{5,6},{6,7},{7,8},{8,9},{9,10},{10,1... | collective-permute-start | bytes 2359304 | tf_op jit(solution)/shard_map/ppermute | solution.py:194
  14.9 20.8 %copy-start.3 = (bf16[4,384,128]{2,1,0:T(8,128)(2,1)}, bf16[4,384,128]{2,1,0:T(8,128)(2,1)S(1)}, u32[]{:S(2)}) copy-start(bf16[4,384,128]{2,1,0:T(8,128)(2,1)S(1)} %get-tuple-element.17.vb_ref) | copy-start | bytes 1179652
  14.9 20.8 %copy-start.5 = (bf16[4,384,128]{2,1,0:T(8,128)(2,1)}, bf16[4,384,128]{2,1,0:T(8,128)(2,1)S(1)}, u32[]{:S(2)}) copy-start(bf16[4,384,128]{2,1,0:T(8,128)(2,1)S(1)} %get-tuple-element.18.kb_ref) | copy-start | bytes 1179652
  15.6 20.2 %copy-start.7 = (bf16[4,384,128]{2,1,0:T(8,128)(2,1)}, bf16[4,384,128]{2,1,0:T(8,128)(2,1)S(1)}, u32[]{:S(2)}) copy-start(bf16[4,384,128]{2,1,0:T(8,128)(2,1)S(1)} %get-tuple-element.19.va_ref) | copy-start | bytes 1179652
  15.6 20.2 %copy-start.9 = (bf16[4,384,128]{2,1,0:T(8,128)(2,1)}, bf16[4,384,128]{2,1,0:T(8,128)(2,1)S(1)}, u32[]{:S(2)}) copy-start(bf16[4,384,128]{2,1,0:T(8,128)(2,1)S(1)} %get-tuple-element.20.ka_ref) | copy-start | bytes 1179652
  35.8 0.6 copy-start.14
  36.4 10.1 %collective-permute-start.3 = (bf16[1536,128]{1,0:T(8,128)(2,1)S(1)}, bf16[1536,128]{1,0:T(8,128)(2,1)S(1)}, u32[]{:S(2)}, u32[]{:S(2)}) collective-permute-start(bf16[1536,128]{1,0:T(8,128)(2,1)S(1)} %bitcast.48), channel_id=1, source_target_pairs={{0,128},{128,0},{1,129},{129,1},{2,130},{130,2},{3,131},{131,3},{4... | collective-permute-start | bytes 1179656 | tf_op jit(solution)/shard_map/ppermute | solution.py:198
  38.7 7.8 %collective-permute-start.2 = (bf16[128,768]{1,0:T(8,128)(2,1)S(1)}, bf16[128,768]{1,0:T(8,128)(2,1)S(1)}, u32[]{:S(2)}, u32[]{:S(2)}) collective-permute-start(bf16[128,768]{1,0:T(8,128)(2,1)S(1)} %constant_dynamic-slice_fusion), channel_id=1, source_target_pairs={{0,128},{128,0},{1,129},{129,1},{2,130},{130,2},{3,131},{131,3},{4... | collective-permute-start | bytes 589832 | tf_op jit(solution)/shard_map/ppermute | solution.py:198
  46.5 2.2 %copy-start.18 = (bf16[1536,128]{1,0:T(8,128)(2,1)}, bf16[1536,128]{1,0:T(8,128)(2,1)S(1)}, u32[]{:S(2)}) copy-start(bf16[1536,128]{1,0:T(8,128)(2,1)S(1)} %collective-permute-done.3) | copy-start | bytes 1179652
  54.4 2.9 %copy-start.16 = (bf16[768,1536]{1,0:T(8,128)(2,1)S(1)}, bf16[768,1536]{1,0:T(8,128)(2,1)}, u32[]{:S(2)}) copy-start(bf16[768,1536]{1,0:T(8,128)(2,1)} %all-gather.2.cloned.1.call-done) | copy-start | bytes 7077892
  56.7 10.7 %collective-permute-start.4 = (bf16[1536,128]{0,1:T(8,128)(2,1)S(1)}, bf16[1536,128]{0,1:T(8,128)(2,1)S(1)}, u32[]{:S(2)}, u32[]{:S(2)}) collective-permute-start(bf16[1536,128]{0,1:T(8,128)(2,1)S(1)} %fusion), channel_id=1, source_target_pairs={{0,128},{128,0},{1,129},{129,1},{2,130},{130,2},{3,131},{131,3},{4... | collective-permute-start | bytes 1179656 | tf_op jit(solution)/shard_map/ppermute | solution.py:198
  67.7 1.0 copy-start.4
  68.7 1.0 copy-start.6
  69.7 1.0 copy-start.8
  70.7 1.0 copy-start.10
  71.7 1.0 copy-start.12
  72.7 0.8 copy-start.15
  73.5 46.4 %copy-start.17 = (bf16[768,1536]{1,0:T(8,128)(2,1)S(1)}, bf16[768,1536]{1,0:T(8,128)(2,1)}, u32[]{:S(2)}) copy-start(bf16[768,1536]{1,0:T(8,128)(2,1)} %all-gather.2.cloned.1.call-done) | copy-start | bytes 7077892
  73.5 46.4 %copy-start.19 = (bf16[1536,128]{1,0:T(8,128)(2,1)S(1)}, bf16[1536,128]{1,0:T(8,128)(2,1)}, u32[]{:S(2)}) copy-start(bf16[1536,128]{1,0:T(8,128)(2,1)} %copy-done.18) | copy-start | bytes 1179652
  73.5 46.4 %copy-start.20 = (bf16[128,768]{1,0:T(8,128)(2,1)S(1)}, bf16[128,768]{1,0:T(8,128)(2,1)}, u32[]{:S(2)}) copy-start(bf16[128,768]{1,0:T(8,128)(2,1)} %convolution_convert_fusion.2) | copy-start | bytes 589828
  92.5 67.7 %collective-permute-start.5 = (bf16[2,4,384,128]{3,2,1,0:T(8,128)(2,1)}, bf16[2,4,384,128]{3,2,1,0:T(8,128)(2,1)}, u32[]{:S(2)}, u32[]{:S(2)}) collective-permute-start(bf16[2,4,384,128]{3,2,1,0:T(8,128)(2,1)} %get-tuple-element.15), channel_id=1, source_target_pairs={{1,0},{2,1},{3,2},{4,3},{5,4},{6,5},{7,6},{8,7},{9,8},{10,9},{11,1... | collective-permute-start | bytes 2359304 | tf_op jit(solution)/shard_map/ppermute | solution.py:194
  93.8 66.4 %collective-permute-start.6 = (bf16[2,4,384,128]{3,2,1,0:T(8,128)(2,1)}, bf16[2,4,384,128]{3,2,1,0:T(8,128)(2,1)}, u32[]{:S(2)}, u32[]{:S(2)}) collective-permute-start(bf16[2,4,384,128]{3,2,1,0:T(8,128)(2,1)} %get-tuple-element.16), channel_id=1, source_target_pairs={{0,1},{1,2},{2,3},{3,4},{4,5},{5,6},{6,7},{7,8},{8,9},{9,10},{10,1... | collective-permute-start | bytes 2359304 | tf_op jit(solution)/shard_map/ppermute | solution.py:194
  151.9 8.4 %collective-permute-start.7 = (f32[96,128]{1,0:T(8,128)S(1)}, f32[96,128]{1,0:T(8,128)S(1)}, u32[]{:S(2)}, u32[]{:S(2)}) collective-permute-start(f32[96,128]{1,0:T(8,128)S(1)} %convert_reduce_fusion), channel_id=1, source_target_pairs={{0,0},{4,4},{8,128},{12,132},{128,8},{132,12},{136,136},{140,140},... | collective-permute-start | bytes 147464 | tf_op jit(solution)/shard_map/ppermute | solution.py:245
Sparse Core Ops, SparseCore 0:
  9.8 44.5 all-gather.1
  57.5 67.0 reduce-scatter.1
